TPU v7x, 32 devices: a whole 2x2x4 slice. The times are simulated.
32 devices in a mesh: groups: 2 (over y), outer: 4 (over z), inner: 4 (over x, core).
Axes of the slice: x: 2, y: 2, z: 4, core: 2. Of those that a mesh axis runs over, the one named last changes fastest.
Arguments:
- initial_state: float32 [768], P('groups'), parts along dimension 0, may hold values from -6 to 6
- duty_codes: int32 [256], P(('groups', 'outer', 'inner')), parts along dimension 0, may hold values from 0 to 15
- dwell_counts: int32 [256], P(('groups', 'outer', 'inner')), parts along dimension 0, may hold values from 1 to 8
- coupling: float32 [2, 384, 384], replicated, as said below
- decay_rates: float32 [384], replicated, may hold values from 1e-05 to 0.03
- drive_on: float32 [384], replicated, may hold values from -0.02 to 0.02
- drive_off: float32 [384], replicated, may hold values from -0.02 to 0.02
Outputs:
- end_states: float32 [256, 384], P(('groups', 'outer', 'inner')), parts along dimension 0
There are 2 independent parts, one for each index of `groups`. A program takes and returns all parts, laid end to end along the dimension named above; an argument that names none is the same for every part. Nothing has to cross between parts.
Inputs may be any that keep to these rules, and one draw needn't show every extreme that they name: coupling[0] and coupling[1] are each antisymmetric (the transpose of coupling[k] is minus coupling[k]); every entry lies within plus or minus 0.068 / sqrt(768), and that bound is reached.
All inputs are finite; a program needn't handle non-finite values.
Results may differ from a plain program's by a relative error of at most 0.00026.
Values sent between devices are 32-bit elements; how exact they have to be, the bound alone decides.
A program may use at most 128 MiB of HBM per device.

v0:
```python
import jax
import jax.numpy as jnp
from jax import lax
from jax.sharding import PartitionSpec as P

DUTY_LEVELS = 16
DWELL_MAX = 8


def prefix(value, axis, join, neutral):
    count, mine = (lax.axis_size(axis), lax.axis_index(axis))
    pieces = jax.tree.map(lambda part: lax.all_gather(part, axis), value)
    total = jax.tree.map(
        lambda part, zero: jnp.full_like(part, 0) + jnp.asarray(zero, part.dtype), value, neutral
    )

    def turn(position, total):
        longer = join(total, jax.tree.map(lambda part: part[position], pieces))
        return jax.tree.map(lambda new, old: jnp.where(position < mine, new, old), longer, total)

    return lax.fori_loop(0, count - 1, turn, total)


def from_root(value, axis, source):
    kept = jnp.where(lax.axis_index(axis) == source, value, 0).astype(value.dtype)
    return lax.psum(kept, axis)


def matmul(left, right):
    return jnp.dot(left, right, precision=lax.Precision.HIGHEST)


def combine(earlier, later):
    return (matmul(later[0], earlier[0]), matmul(later[0], earlier[1]) + later[1])


def build_step(codes, coupling, decay_rates, drive_on, drive_off, identity):
    duty, dwell = codes
    frac = (duty.astype(jnp.float32) + 0.5) / DUTY_LEVELS
    counts = dwell.astype(jnp.float32)
    keep = jnp.exp(-counts * decay_rates)
    mixing = identity + frac * coupling[0] + (1.0 - frac) * coupling[1]
    matrix = keep[:, None] * mixing
    offset = counts / DWELL_MAX * (frac * drive_on + (1.0 - frac) * drive_off)
    return (matrix, offset)


def on_device(initial_state, duty_codes, dwell_counts, coupling, decay_rates, drive_on, drive_off):
    width = initial_state.shape[0]
    identity = jnp.eye(width, dtype=jnp.float32)
    zeros = jnp.zeros((width,), jnp.float32)

    def compose(carry, codes):
        matrix, offset = build_step(codes, coupling, decay_rates, drive_on, drive_off, identity)
        return ((matmul(matrix, carry[0]), matmul(matrix, carry[1]) + offset), None)

    local_map, unused = lax.scan(compose, (identity, zeros), (duty_codes, dwell_counts))
    product, shifted = local_map
    inner_map = prefix((product, shifted), "inner", combine, (identity, zeros))
    through = combine(inner_map, (product, shifted))
    last_one = lax.axis_size("inner") - 1
    block_map = (from_root(through[0], "inner", last_one), from_root(through[1], "inner", last_one))
    outer_map = prefix((block_map[0], block_map[1]), "outer", combine, (identity, zeros))
    block_start = matmul(outer_map[0], initial_state) + outer_map[1]
    state = matmul(inner_map[0], block_start) + inner_map[1]

    def advance(current, codes):
        matrix, offset = build_step(codes, coupling, decay_rates, drive_on, drive_off, identity)
        nxt = matmul(matrix, current) + offset
        return (nxt, nxt)

    final, results = lax.scan(advance, state, (duty_codes, dwell_counts))
    return results


def solution(mesh):
    return jax.shard_map(
        on_device,
        mesh=mesh,
        in_specs=(
            P("groups"),
            P(("groups", "outer", "inner")),
            P(("groups", "outer", "inner")),
            P(),
            P(),
            P(),
            P(),
        ),
        out_specs=P(("groups", "outer", "inner"), None),
        check_vma=False,
    )
```

profile of v0, /device:TPU:0, one launch (start us, length us, event | category | flops | bytes accessed | tf_op | source)
XLA Modules:
  0.0 265.3 jit_solution(14353439623340669262)
XLA Ops:
  6.6 72.2 %while.59 = (s32[]{:T(128)}, f32[384,384]{1,0:T(8,128)S(1)}, f32[384]{0:T(512)S(1)}, s32[8]{0:T(128)}, f32[384]{0:T(512)}, /*index=5*/s32[8]{0:T(128)}, f32[2,38...) while((s32[]{:T(128)}, f32[384,384]{1,0:T(8,128)S(1)}, ...), condition=%wide.region_1.2_spmd.clone, body=%wide.region_0.1_spmd.clone.sunk | while | flops 683313792 | bytes 9458995 | solution.py:57
  6.7 1.4 dynamic_slice.80
  11.5 2.0 convolution_reduce_fusion.12
  14.3 1.4 fusion.68
  15.7 1.4 dynamic_slice.80
  20.5 2.0 convolution_reduce_fusion.12
  23.3 1.4 fusion.68
  24.7 1.4 dynamic_slice.80
  29.6 2.0 convolution_reduce_fusion.12
  32.3 1.4 fusion.68
  33.7 1.4 dynamic_slice.80
  38.6 2.0 convolution_reduce_fusion.12
  41.4 1.4 fusion.68
  42.8 1.4 dynamic_slice.80
  47.6 2.0 convolution_reduce_fusion.12
  50.4 1.4 fusion.68
  51.8 1.4 dynamic_slice.80
  56.6 2.0 convolution_reduce_fusion.12
  59.4 1.4 fusion.68
  60.8 1.4 dynamic_slice.80
  65.7 2.0 convolution_reduce_fusion.12
  68.4 1.4 fusion.68
  69.8 1.4 dynamic_slice.80
  74.7 2.0 convolution_reduce_fusion.12
  77.5 1.4 fusion.68
  79.8 6.1 %all-gather.2 = f32[4,1,384]{2,1,0:T(1,128)S(1)} all-gather(f32[1,1,384]{2,1,0:T(1,128)S(1)} %reshape.36), channel_id=3, replica_groups=mesh['groups'=2,'outer'=4,'inner'=4] {'inner'}, dimensions={0}, use_global_device_ids=true | all-gather | bytes 7680 | tf_op jit(solution)/shard_map/all_gather | solution.py:12
  85.9 20.7 %all-gather.9.cloned.1.call-done = f32[1536,384]{1,0:T(8,128)} async-done(((f32[384,384]{1,0:T(8,128)}), f32[1536,384]{1,0:T(8,128)}) %all-gather.9.cloned.1.call-update) | async-done | bytes 2359312 | tf_op jit(solution)/shard_map/all_gather | solution.py:12
  106.6 12.6 %while.60 = (s32[]{:T(128)}, f32[384,384]{1,0:T(8,128)S(1)}, f32[384]{0:T(512)S(1)}, s32[]{:T(128)}, f32[4,384,384]{2,1,0:T(8,128)}, /*index=5*/f32[4,384]{1,0:T(4,128)S(1)}, s32[]{:T(128)}, s32[]{:T(128)}) while((s32[]{:T(128)}, f32[384,384]{1,0:T(8,128)S(1)}, f32[384]{0:T(512)S(1)}, s32[]{:T(128)}, f32[4,384,384]{2,1,0:T(8,128)}, ...), condition=%wide.region_3.4_spmd.clone, body=%wide.region_2.3_spmd.clone.sunk | while | flops 681395712 | bytes 4148335 | solution.py:21
  106.6 1.8 convolution_reduce_fusion.13
  108.5 2.3 convolution_select_fusion.5
  110.9 1.7 convolution_reduce_fusion.13
  112.7 2.3 convolution_select_fusion.5
  115.1 1.7 convolution_reduce_fusion.13
  116.9 2.3 convolution_select_fusion.5
  119.3 2.1 fusion.30
  121.4 33.6 %all-reduce.2.cloned.1.call-done = f32[1,384,384]{2,1,0:T(8,128)} async-done(((f32[1,384,384]{2,1,0:T(8,128)}), f32[1,384,384]{2,1,0:T(8,128)}) %all-reduce.2.cloned.1.call-update) | async-done | bytes 589840 | tf_op jit(solution)/shard_map/psum | solution.py:26
  155.8 5.8 %psum.15 = f32[1,384]{1,0:T(1,128)S(1)} all-reduce(f32[1,384]{1,0:T(1,128)S(1)} %all_gather.30), channel_id=1, replica_groups=mesh['groups'=2,'outer'=4,'inner'=4] {'inner'}, use_global_device_ids=true, to_apply=%region_5.6 | all-reduce | flops 384 | bytes 3072 | tf_op jit(solution)/shard_map/psum | solution.py:26
  161.5 12.2 %all-gather.3 = f32[4,1,384]{2,1,0:T(1,128)S(1)} all-gather(f32[1,1,384]{2,1,0:T(1,128)S(1)} %bitcast.112), channel_id=1, replica_groups=mesh['groups'=2,'outer'=4,'inner'=4] {'outer'}, dimensions={0}, use_global_device_ids=true | all-gather | bytes 7680 | tf_op jit(solution)/shard_map/all_gather | solution.py:12
  173.7 33.4 %all-gather.7.cloned.1.call-done = f32[4,384,384]{2,1,0:T(8,128)} async-done(((f32[1,384,384]{2,1,0:T(8,128)}), f32[4,384,384]{2,1,0:T(8,128)}) %all-gather.7.cloned.1.call-update) | async-done | bytes 2359312 | tf_op jit(solution)/shard_map/all_gather | solution.py:12
  207.2 12.7 %while.61 = (s32[]{:T(128)}, f32[384,384]{1,0:T(8,128)S(1)}, f32[384]{0:T(512)S(1)}, s32[]{:T(128)}, f32[4,384,384]{2,1,0:T(8,128)}, /*index=5*/f32[4,384]{1,0:T(4,128)S(1)}, s32[]{:T(128)}, s32[]{:T(128)}) while((s32[]{:T(128)}, f32[384,384]{1,0:T(8,128)S(1)}, f32[384]{0:T(512)S(1)}, s32[]{:T(128)}, f32[4,384,384]{2,1,0:T(8,128)}, ...), condition=%wide.region_7.8_spmd.clone, body=%wide.region_6.7_spmd.clone.sunk | while | flops 681395712 | bytes 4148335 | solution.py:21
  207.2 1.8 convolution_reduce_fusion.14
  209.1 2.3 convolution_select_fusion.6
  211.5 1.7 convolution_reduce_fusion.14
  213.3 2.3 convolution_select_fusion.6
  215.7 1.7 convolution_reduce_fusion.14
  217.5 2.3 convolution_select_fusion.6
  221.3 37.5 %while.58 = (s32[]{:T(128)}, f32[384]{0:T(512)S(1)}, f32[8,384]{1,0:T(8,128)}, s32[8]{0:T(128)S(1)}, f32[384]{0:T(512)S(1)}, /*index=5*/s32[8]{0:T(128)S(1)}, f3...) while((s32[]{:T(128)}, f32[384]{0:T(512)S(1)}, ...), condition=%wide.region_9.10_spmd.clone, body=%wide.region_8.9_spmd.clone.sunk | while | flops 2803977 | bytes 1202953 | solution.py:72
  224.7 1.3 dynamic_update_slice.6
  (193 shorter events, 51.5 us)
Async XLA Ops:
  6.5 100.1 %all-gather.9.cloned.1.call-start = ((), (), s32[]{:S(2)}) async-start(), calls=%async_computation.2 | async-start | bytes 2949120 | tf_op jit(solution)/shard_map/all_gather | solution.py:12
  6.6 7.6 %copy-start.2 = (f32[2,384,384]{2,1,0:T(8,128)S(1)}, f32[2,384,384]{2,1,0:T(8,128)}, u32[]{:S(2)}) copy-start(f32[2,384,384]{2,1,0:T(8,128)} %get-tuple-element.717) | copy-start | bytes 3538948 | tf_op jit(solution)/shard_map/while
  15.7 7.6 %copy-start.2 = (f32[2,384,384]{2,1,0:T(8,128)S(1)}, f32[2,384,384]{2,1,0:T(8,128)}, u32[]{:S(2)}) copy-start(f32[2,384,384]{2,1,0:T(8,128)} %get-tuple-element.717) | copy-start | bytes 3538948 | tf_op jit(solution)/shard_map/while
  24.7 7.6 %copy-start.2 = (f32[2,384,384]{2,1,0:T(8,128)S(1)}, f32[2,384,384]{2,1,0:T(8,128)}, u32[]{:S(2)}) copy-start(f32[2,384,384]{2,1,0:T(8,128)} %get-tuple-element.717) | copy-start | bytes 3538948 | tf_op jit(solution)/shard_map/while
  33.7 7.6 %copy-start.2 = (f32[2,384,384]{2,1,0:T(8,128)S(1)}, f32[2,384,384]{2,1,0:T(8,128)}, u32[]{:S(2)}) copy-start(f32[2,384,384]{2,1,0:T(8,128)} %get-tuple-element.717) | copy-start | bytes 3538948 | tf_op jit(solution)/shard_map/while
  42.7 7.6 %copy-start.2 = (f32[2,384,384]{2,1,0:T(8,128)S(1)}, f32[2,384,384]{2,1,0:T(8,128)}, u32[]{:S(2)}) copy-start(f32[2,384,384]{2,1,0:T(8,128)} %get-tuple-element.717) | copy-start | bytes 3538948 | tf_op jit(solution)/shard_map/while
  51.8 7.6 %copy-start.2 = (f32[2,384,384]{2,1,0:T(8,128)S(1)}, f32[2,384,384]{2,1,0:T(8,128)}, u32[]{:S(2)}) copy-start(f32[2,384,384]{2,1,0:T(8,128)} %get-tuple-element.717) | copy-start | bytes 3538948 | tf_op jit(solution)/shard_map/while
  60.8 7.6 %copy-start.2 = (f32[2,384,384]{2,1,0:T(8,128)S(1)}, f32[2,384,384]{2,1,0:T(8,128)}, u32[]{:S(2)}) copy-start(f32[2,384,384]{2,1,0:T(8,128)} %get-tuple-element.717) | copy-start | bytes 3538948 | tf_op jit(solution)/shard_map/while
  69.8 7.6 %copy-start.2 = (f32[2,384,384]{2,1,0:T(8,128)S(1)}, f32[2,384,384]{2,1,0:T(8,128)}, u32[]{:S(2)}) copy-start(f32[2,384,384]{2,1,0:T(8,128)} %get-tuple-element.717) | copy-start | bytes 3538948 | tf_op jit(solution)/shard_map/while
  78.8 0.8 copy-start
  79.7 75.3 %all-reduce.2.cloned.1.call-start = ((), (), s32[]{:S(2)}) async-start(), calls=%async_computation | async-start | bytes 1179648 | tf_op jit(solution)/shard_map/psum | solution.py:26
  106.6 12.6 %copy-start.1 = (f32[384,384]{1,0:T(8,128)S(1)}, f32[384,384]{1,0:T(8,128)}, u32[]{:S(2)}) copy-start(f32[384,384]{1,0:T(8,128)} %copy-done) | copy-start | bytes 1769476
  119.2 35.8 %copy-start.7 = (f32[384]{0:T(512)S(1)}, f32[384]{0:T(512)}, u32[]{:S(2)}) copy-start(f32[384]{0:T(512)} %param.15) | copy-start | bytes 4612
  121.4 85.8 %all-gather.7.cloned.1.call-start = ((), (), s32[]{:S(2)}) async-start(), calls=%async_computation.1 | async-start | bytes 2949120 | tf_op jit(solution)/shard_map/all_gather | solution.py:12
  207.2 14.1 %copy-start.3 = (f32[2,384,384]{2,1,0:T(8,128)S(1)}, f32[2,384,384]{2,1,0:T(8,128)}, u32[]{:S(2)}) copy-start(f32[2,384,384]{2,1,0:T(8,128)} %get-tuple-element.826) | copy-start | bytes 3538948
  207.2 14.1 %copy-start.4 = (f32[384]{0:T(512)S(1)}, f32[384]{0:T(512)}, u32[]{:S(2)}) copy-start(f32[384]{0:T(512)} %get-tuple-element.832) | copy-start | bytes 4612
  207.2 14.1 %copy-start.5 = (f32[384]{0:T(512)S(1)}, f32[384]{0:T(512)}, u32[]{:S(2)}) copy-start(f32[384]{0:T(512)} %get-tuple-element.833) | copy-start | bytes 4612
  207.2 14.1 %copy-start.6 = (f32[384]{0:T(512)S(1)}, f32[384]{0:T(512)}, u32[]{:S(2)}) copy-start(f32[384]{0:T(512)} %get-tuple-element.834) | copy-start | bytes 4612
  207.2 14.1 %copy-start.8 = (s32[8]{0:T(128)S(1)}, s32[8]{0:T(128)}, u32[]{:S(2)}) copy-start(s32[8]{0:T(128)} %get-tuple-element.836) | copy-start | bytes 100
  207.2 14.1 %copy-start.9 = (s32[8]{0:T(128)S(1)}, s32[8]{0:T(128)}, u32[]{:S(2)}) copy-start(s32[8]{0:T(128)} %get-tuple-element.837) | copy-start | bytes 100
Sparse Core Ops, SparseCore 0:
  79.8 26.7 all-gather.8
  121.5 33.4 all-reduce.1
  156.6 50.5 all-gather.6
where the time goes:
time: 267 us; the launch traced here: 265 us
  waiting for transfers between devices  87.8 us (33%)
  matrix products  61.9 us (23%)
  local copies, waits for them, and re-layouts  44.3 us (17%)
  blocking collectives  24.1 us (9%)
  loops' own time  22.4 us (8%)
  between operations  13.4 us (5%)
  other arithmetic  11.5 us (4%)
    dot_general x40, matrix products, matmul(): return jnp.dot(left, right, precision=lax.Precision.HIGHEST)  61.9 us
    all_gather x2, waiting for transfers between devices, prefix(): pieces = jax.tree.map(lambda part: lax.all_gather(part, axis), value)  54.1 us
    psum x1, waiting for transfers between devices, from_root(): return lax.psum(kept, axis)  33.6 us
    dynamic_slice x32, local copies, waits for them, and re-layouts, on_device(): lax.scan(compose, (identity, zeros), (duty_codes, dwell_counts))  31.9 us
    all_gather x2, blocking collectives, prefix(): pieces = jax.tree.map(lambda part: lax.all_gather(part, axis), value)  18.3 us
    another operation x1, loops' own time, on_device(): lax.scan(compose, (identity, zeros), (duty_codes, dwell_counts))  11.7 us
    dynamic_update_slice x8, local copies, waits for them, and re-layouts, on_device(): final, results = lax.scan(advance, state, (duty_codes, dwell_counts))  10.6 us
    another operation x1, loops' own time, on_device(): final, results = lax.scan(advance, state, (duty_codes, dwell_counts))  10.4 us
  transfers between devices with their start and end apart: 3, of which 3 were waited for; matrix products, arithmetic and copies ran while one was open for 0% of the time, Pallas kernels for 0%

commit v1 on v0

v1 whole, which is shorter than its diff:
```python
import functools
import jax
import jax.numpy as jnp
from jax import lax
from jax.experimental import pallas as pl
from jax.experimental.pallas import tpu as pltpu
from jax.sharding import PartitionSpec as P

DUTY_LEVELS = 16
DWELL_MAX = 8
LANES = 128
SUB = 8


def replay(axes, local, codes, x0, coupling, decay_col, decay_row, on_col, on_row, off_col, off_row,
           out, plus, minus, keep_col, keep_row, drive_col, drive_row):
    width = x0.shape[1]
    blocks = width // LANES
    me = lax.axis_index(axes)
    row_id = lax.broadcasted_iota(jnp.int32, (width, width), 0)
    col_id = lax.broadcasted_iota(jnp.int32, (width, width), 1)

    def tabulate_duty(level, unused):
        frac = (level.astype(jnp.float32) + 0.5) / DUTY_LEVELS
        mixing = frac * coupling[0] + (1.0 - frac) * coupling[1]
        eye = jnp.where(row_id == col_id, 1.0, 0.0).astype(jnp.float32)
        plus[level] = eye + mixing
        minus[level] = eye - mixing
        drive_col[level] = jnp.broadcast_to(frac * on_col[...] + (1.0 - frac) * off_col[...], (width, LANES))
        drive_row[level] = jnp.broadcast_to(frac * on_row[...] + (1.0 - frac) * off_row[...], (SUB, width))
        return 0

    lax.fori_loop(0, DUTY_LEVELS, tabulate_duty, 0)

    def tabulate_dwell(level, unused):
        count = level.astype(jnp.float32) + 1.0
        keep_col[level] = jnp.broadcast_to(jnp.exp(-count * decay_col[...]), (width, LANES))
        keep_row[level] = jnp.broadcast_to(jnp.exp(-count * decay_row[...]), (SUB, width))
        return 0

    lax.fori_loop(0, DWELL_MAX, tabulate_dwell, 0)
    diag = (lax.broadcasted_iota(jnp.int32, (LANES, LANES), 0)
            == lax.broadcasted_iota(jnp.int32, (LANES, LANES), 1))

    def two_steps(first, state, place):
        duty_a, duty_b = codes[0, first], codes[0, first + 1]
        dwell_a, dwell_b = codes[1, first], codes[1, first + 1]
        scale_a = dwell_a.astype(jnp.float32) / DWELL_MAX
        scale_b = dwell_b.astype(jnp.float32) / DWELL_MAX
        parts = [state[:, LANES * k:LANES * (k + 1)] for k in range(blocks)]
        sums = [[None, None] for k in range(blocks)]
        columns = []
        for r in range(width // SUB):
            rows = slice(SUB * r, SUB * (r + 1))
            term = plus[duty_a, rows, 0:LANES] * parts[0]
            for k in range(1, blocks):
                term = term + plus[duty_a, rows, LANES * k:LANES * (k + 1)] * parts[k]
            total = jnp.sum(term, axis=1, keepdims=True)
            middle = keep_col[dwell_a - 1, rows] * total + scale_a * drive_col[duty_a, rows]
            if place is not None:
                columns.append(middle)
            for k in range(blocks):
                term = minus[duty_b, rows, LANES * k:LANES * (k + 1)] * middle
                sums[k][r % 2] = term if sums[k][r % 2] is None else sums[k][r % 2] + term
        flat = jnp.concatenate([jnp.sum(s[0] + s[1], axis=0, keepdims=True) for s in sums], axis=1)
        after = keep_row[dwell_b - 1] * jnp.broadcast_to(flat, (SUB, width)) + scale_b * drive_row[duty_b]
        if place is not None:
            per = LANES // SUB
            for k in range(blocks):
                square = jnp.concatenate(columns[per * k:per * (k + 1)], axis=0)
                out[place:place + 1, LANES * k:LANES * (k + 1)] = jnp.sum(
                    jnp.where(diag, square, 0.0), axis=0, keepdims=True)
            out[place + 1:place + 2, :] = after[0:1]
        return after

    state = jnp.broadcast_to(x0[...], (SUB, width))
    state = lax.fori_loop(0, me * (local // 2), lambda pair, state: two_steps(2 * pair, state, None), state)
    for step in range(0, local, 2):
        state = two_steps(me * local + step, state, step)


def on_device(initial_state, duty_codes, dwell_counts, coupling, decay_rates, drive_on, drive_off):
    width, local = initial_state.shape[0], duty_codes.shape[0]
    axes = ("outer", "inner")
    codes = lax.all_gather(jnp.stack([duty_codes, dwell_counts]), axes, axis=1, tiled=True)
    scratch = [
        pltpu.VMEM((DUTY_LEVELS, width, width), jnp.float32),
        pltpu.VMEM((DUTY_LEVELS, width, width), jnp.float32),
        pltpu.VMEM((DWELL_MAX, width, LANES), jnp.float32),
        pltpu.VMEM((DWELL_MAX, SUB, width), jnp.float32),
        pltpu.VMEM((DUTY_LEVELS, width, LANES), jnp.float32),
        pltpu.VMEM((DUTY_LEVELS, SUB, width), jnp.float32),
    ]
    return pl.pallas_call(
        functools.partial(replay, axes, local),
        out_shape=jax.ShapeDtypeStruct((local, width), jnp.float32),
        in_specs=[pl.BlockSpec(memory_space=pltpu.SMEM)] + [pl.BlockSpec(memory_space=pltpu.VMEM)] * 8,
        out_specs=pl.BlockSpec(memory_space=pltpu.VMEM),
        scratch_shapes=scratch,
        compiler_params=pltpu.CompilerParams(vmem_limit_bytes=48 * 2**20),
    )(codes, initial_state[None, :], coupling, decay_rates[:, None], decay_rates[None, :],
      drive_on[:, None], drive_on[None, :], drive_off[:, None], drive_off[None, :])


def solution(mesh):
    return jax.shard_map(
        on_device,
        mesh=mesh,
        in_specs=(
            P("groups"),
            P(("groups", "outer", "inner")),
            P(("groups", "outer", "inner")),
            P(),
            P(),
            P(),
            P(),
        ),
        out_specs=P(("groups", "outer", "inner"), None),
        check_vma=False,
    )
```

time: 267 us -> 41.1 us (0.15)
  the two profiles are of different devices: /device:TPU:0 before, /device:TPU:31 now
where the time goes in v1:
time: 41.1 us; the launch traced here: 40.7 us
  blocking collectives  16.8 us (41%)
  Pallas kernels  16.7 us (41%)
  local copies, waits for them, and re-layouts  6.46 us (16%)
  other arithmetic  0.68 us (2%)
    all_gather x1, blocking collectives, on_device(): lax.all_gather(jnp.stack([duty_codes, dwell_counts]), axes, axis=1, tiled...  16.8 us
    pallas_call x1, Pallas kernels, on_device(): pl.pallas_call(functools.partial(replay, axes, local), out_shape=jax.Shap...  16.7 us
    unnamed x3, local copies, waits for them, and re-layouts  1.36 us

profile of v1, /device:TPU:31, one launch (start us, length us, event | category | flops | bytes accessed | tf_op | source)
XLA Modules:
  0.0 40.7 jit_solution(14533426037815184739)
XLA Ops:
  0.0 0.7 %add_bitcast_fusion = s32[1,8,2]{1,2,0:T(2,128)S(1)} fusion(s32[1,8]{1,0:T(1,128)} %bitcast.10, s32[1,8]{1,0:T(1,128)} %bitcast.11), kind=kLoop, calls=%fused_computation | loop fusion | flops 16 | bytes 128
  0.7 0.7 %broadcast_in_dim.21.x0 = f32[1,384]{1,0:T(1,128)S(1)} reshape(f32[384]{0:T(512)} %param.7) | data formatting | bytes 3072 | tf_op jit(solution)/shard_map/broadcast_in_dim | solution.py:101
  1.4 0.7 %broadcast_in_dim.23.decay_row = f32[1,384]{1,0:T(1,128)S(1)} reshape(f32[384]{0:T(512)} %param.11) | data formatting | bytes 3072 | tf_op jit(solution)/shard_map/broadcast_in_dim | solution.py:101
  2.0 0.7 %broadcast_in_dim.25.on_row = f32[1,384]{1,0:T(1,128)S(1)} reshape(f32[384]{0:T(512)} %param.12) | data formatting | bytes 3072 | tf_op jit(solution)/shard_map/broadcast_in_dim | solution.py:102
  2.7 0.7 %broadcast_in_dim.27.off_row = f32[1,384]{1,0:T(1,128)S(1)} reshape(f32[384]{0:T(512)} %param.13) | data formatting | bytes 3072 | tf_op jit(solution)/shard_map/broadcast_in_dim | solution.py:102
  3.4 16.8 %all-gather = s32[16,8,2]{1,2,0:T(2,128)S(1)} all-gather(s32[1,8,2]{1,2,0:T(2,128)S(1)} %add_bitcast_fusion), channel_id=1, replica_groups=mesh['groups'=2,'outer'=4,'inner'=4] {'outer','inner'}, dimensions={0}, use_global_device_ids=true | all-gather | bytes 1088 | tf_op jit(solution)/shard_map/all_gather | solution.py:85
  20.3 0.1 reshape.1
  20.3 0.8 %broadcast_in_dim.28.decay_col = f32[384,1]{1,0:T(8,128)S(1)} reshape(f32[384]{0:T(512)} %param.11) | data formatting | bytes 3072 | tf_op jit(solution)/shard_map/broadcast_in_dim | solution.py:101
  21.1 0.8 %broadcast_in_dim.29.on_col = f32[384,1]{1,0:T(8,128)S(1)} reshape(f32[384]{0:T(512)} %param.12) | data formatting | bytes 3072 | tf_op jit(solution)/shard_map/broadcast_in_dim | solution.py:102
  21.9 0.8 %broadcast_in_dim.30.off_col = f32[384,1]{1,0:T(8,128)S(1)} reshape(f32[384]{0:T(512)} %param.13) | data formatting | bytes 3072 | tf_op jit(solution)/shard_map/broadcast_in_dim | solution.py:102
  22.7 0.0 copy-start
  22.8 1.3 %copy-done = f32[2,384,384]{2,1,0:T(8,128)S(1)} copy-done((f32[2,384,384]{2,1,0:T(8,128)S(1)}, f32[2,384,384]{2,1,0:T(8,128)}, u32[]{:S(2)}) %copy-start) | copy-done | bytes 1179672
  24.0 16.7 %shard_map.73 = f32[8,384]{1,0:T(8,128)} custom-call(s32[2,128]{1,0:T(2,128)S(1)} %bitcast.9, f32[1,384]{1,0:T(1,128)S(1)} %broadcast_in_dim.21.x0, f32[2,384,384]{2,1,0:T(8,128)S(1)} %copy-done, f32[384,1]{1,0:T(8,128)S(1)} %broadcast_in_dim.28.decay_col, f32[1,384]{1,0:T(1,128)S(1)} %broadcast_in_dim.23.decay_row, f32[384,1]{1,0:T(8,128)S(1)} %broadcast_in_dim.29.on_col, ...), custom_call_target="tpu_custom_call" | custom-call | tf_op jit(solution)/shard_map/pallas_call | solution.py:94
  (1 shorter events, 0.0 us)
Async XLA Ops:
  22.7 1.3 %copy-start = (f32[2,384,384]{2,1,0:T(8,128)S(1)}, f32[2,384,384]{2,1,0:T(8,128)}, u32[]{:S(2)}) copy-start(f32[2,384,384]{2,1,0:T(8,128)} %coupling.1) | copy-start | bytes 3538948

commit v2 on v1

v2 whole, which is shorter than its diff:
```python
import functools
import jax
import jax.numpy as jnp
from jax import lax
from jax.experimental import pallas as pl
from jax.experimental.pallas import tpu as pltpu
from jax.sharding import PartitionSpec as P

DUTY_LEVELS = 16
DWELL_MAX = 8
LANES = 128
SUB = 8


def replay(axes, local, duty, dwell, x0, coupling_hbm, decay, on, off, out,
           plus, minus, keep_col, keep_row, drive_col, drive_row, coupling, packed, landed, codes,
           send_sem, recv_sem, coupling_sem, codes_sem):
    width = x0.shape[0]
    blocks = width // LANES
    inner = lax.axis_size(axes[1])
    count = lax.axis_size(axes[0]) * inner
    me = lax.axis_index(axes)

    def place_of(index):
        return {axes[0]: index // inner, axes[1]: index % inner}

    def push(target):
        return pltpu.make_async_remote_copy(
            src_ref=packed, dst_ref=landed.at[me], send_sem=send_sem.at[target], recv_sem=recv_sem.at[me],
            device_id=place_of(target), device_id_type=pl.DeviceIdType.MESH)

    barrier = pltpu.get_barrier_semaphore()

    def greet(source, unused):
        pl.semaphore_signal(barrier, inc=1, device_id=place_of(source), device_id_type=pl.DeviceIdType.MESH)
        return 0

    lax.fori_loop(0, me, greet, 0)
    load = pltpu.make_async_copy(coupling_hbm, coupling, coupling_sem)
    load.start()
    lane = lax.broadcasted_iota(jnp.int32, (1, LANES), 1)
    line = jnp.zeros((1, LANES), jnp.int32)
    for step in range(local):
        line = jnp.where(lane == step, duty[step], line)
        line = jnp.where(lane == local + step, dwell[step], line)
    packed[...] = line
    landed[me] = line

    @pl.when(me < count - 1)
    def to_later():
        pl.semaphore_wait(barrier, count - 1 - me)

        def send(target, unused):
            push(target).start()
            return 0

        lax.fori_loop(me + 1, count, send, 0)

    load.wait()
    diag = (lax.broadcasted_iota(jnp.int32, (LANES, LANES), 0)
            == lax.broadcasted_iota(jnp.int32, (LANES, LANES), 1))

    def columns_of(row):
        return jnp.concatenate([
            jnp.sum(jnp.where(diag, row[:, LANES * k:LANES * (k + 1)], 0.0), axis=1, keepdims=True)
            for k in range(blocks)], axis=0)

    decay_row, on_row, off_row = (ref[...].reshape(1, width) for ref in (decay, on, off))
    decay_col, on_col, off_col = (columns_of(row) for row in (decay_row, on_row, off_row))
    row_id = lax.broadcasted_iota(jnp.int32, (width, width), 0)
    col_id = lax.broadcasted_iota(jnp.int32, (width, width), 1)

    def tabulate_duty(level, unused):
        frac = (level.astype(jnp.float32) + 0.5) / DUTY_LEVELS
        mixing = frac * coupling[0] + (1.0 - frac) * coupling[1]
        eye = jnp.where(row_id == col_id, 1.0, 0.0).astype(jnp.float32)
        plus[level] = eye + mixing
        minus[level] = eye - mixing
        drive_col[level] = jnp.broadcast_to(frac * on_col + (1.0 - frac) * off_col, (width, LANES))
        drive_row[level] = jnp.broadcast_to(frac * on_row + (1.0 - frac) * off_row, (SUB, width))
        return 0

    lax.fori_loop(0, DUTY_LEVELS, tabulate_duty, 0)

    def tabulate_dwell(level, unused):
        steps = level.astype(jnp.float32)
        keep_col[level] = jnp.broadcast_to(jnp.exp(-steps * decay_col), (width, LANES))
        keep_row[level] = jnp.broadcast_to(jnp.exp(-steps * decay_row), (SUB, width))
        return 0

    lax.fori_loop(0, DWELL_MAX + 1, tabulate_dwell, 0)

    def receive(source, unused):
        pltpu.make_async_remote_copy(
            src_ref=packed, dst_ref=landed.at[source], send_sem=send_sem.at[me], recv_sem=recv_sem.at[source],
            device_id=place_of(source), device_id_type=pl.DeviceIdType.MESH).wait_recv()
        return 0

    lax.fori_loop(0, me, receive, 0)
    unload = pltpu.make_async_copy(landed, codes, codes_sem)
    unload.start()
    unload.wait()

    def two_steps(owner, first, state, place):
        duty_a, duty_b = codes[owner, 0, first], codes[owner, 0, first + 1]
        dwell_a, dwell_b = codes[owner, 0, local + first], codes[owner, 0, local + first + 1]
        scale_a = dwell_a.astype(jnp.float32) / DWELL_MAX
        scale_b = dwell_b.astype(jnp.float32) / DWELL_MAX
        parts = [state[:, LANES * k:LANES * (k + 1)] for k in range(blocks)]
        sums = [[None, None] for k in range(blocks)]
        columns = []
        for r in range(width // SUB):
            rows = slice(SUB * r, SUB * (r + 1))
            term = plus[duty_a, rows, 0:LANES] * parts[0]
            for k in range(1, blocks):
                term = term + plus[duty_a, rows, LANES * k:LANES * (k + 1)] * parts[k]
            total = jnp.sum(term, axis=1, keepdims=True)
            middle = keep_col[dwell_a, rows] * total + scale_a * drive_col[duty_a, rows]
            if place is not None:
                columns.append(middle)
            for k in range(blocks):
                term = minus[duty_b, rows, LANES * k:LANES * (k + 1)] * middle
                sums[k][r % 2] = term if sums[k][r % 2] is None else sums[k][r % 2] + term
        flat = jnp.concatenate([jnp.sum(s[0] + s[1], axis=0, keepdims=True) for s in sums], axis=1)
        after = keep_row[dwell_b] * jnp.broadcast_to(flat, (SUB, width)) + scale_b * drive_row[duty_b]
        if place is not None:
            per = LANES // SUB
            for k in range(blocks):
                square = jnp.concatenate(columns[per * k:per * (k + 1)], axis=0)
                out[place:place + 1, LANES * k:LANES * (k + 1)] = jnp.sum(
                    jnp.where(diag, square, 0.0), axis=0, keepdims=True)
            out[place + 1:place + 2, :] = after[0:1]
        return after

    half = local // 2
    state = jnp.broadcast_to(x0[...].reshape(1, width), (SUB, width))
    state = lax.fori_loop(
        0, me * half, lambda pair, state: two_steps(pair // half, 2 * (pair % half), state, None), state)
    for step in range(0, local, 2):
        state = two_steps(me, step, state, step)

    def finish(target, unused):
        push(target).wait_send()
        return 0

    lax.fori_loop(me + 1, count, finish, 0)


def on_device(initial_state, duty_codes, dwell_counts, coupling, decay_rates, drive_on, drive_off):
    width, local = initial_state.shape[0], duty_codes.shape[0]
    axes = ("outer", "inner")
    count = lax.axis_size(axes[0]) * lax.axis_size(axes[1])
    scratch = [
        pltpu.VMEM((DUTY_LEVELS, width, width), jnp.float32),
        pltpu.VMEM((DUTY_LEVELS, width, width), jnp.float32),
        pltpu.VMEM((DWELL_MAX + 1, width, LANES), jnp.float32),
        pltpu.VMEM((DWELL_MAX + 1, SUB, width), jnp.float32),
        pltpu.VMEM((DUTY_LEVELS, width, LANES), jnp.float32),
        pltpu.VMEM((DUTY_LEVELS, SUB, width), jnp.float32),
        pltpu.VMEM(coupling.shape, jnp.float32),
        pltpu.VMEM((1, LANES), jnp.int32),
        pltpu.VMEM((count, 1, LANES), jnp.int32),
        pltpu.SMEM((count, 1, LANES), jnp.int32),
        pltpu.SemaphoreType.DMA((count,)),
        pltpu.SemaphoreType.DMA((count,)),
        pltpu.SemaphoreType.DMA,
        pltpu.SemaphoreType.DMA,
    ]
    smem, vmem = pl.BlockSpec(memory_space=pltpu.SMEM), pl.BlockSpec(memory_space=pltpu.VMEM)
    return pl.pallas_call(
        functools.partial(replay, axes, local),
        out_shape=jax.ShapeDtypeStruct((local, width), jnp.float32),
        in_specs=[smem, smem, vmem, pl.BlockSpec(memory_space=pl.ANY), vmem, vmem, vmem],
        out_specs=vmem,
        scratch_shapes=scratch,
        compiler_params=pltpu.CompilerParams(
            vmem_limit_bytes=56 * 2**20, collective_id=0, has_side_effects=True),
    )(duty_codes, dwell_counts, initial_state, coupling, decay_rates, drive_on, drive_off)


def solution(mesh):
    return jax.shard_map(
        on_device,
        mesh=mesh,
        in_specs=(
            P("groups"),
            P(("groups", "outer", "inner")),
            P(("groups", "outer", "inner")),
            P(),
            P(),
            P(),
            P(),
        ),
        out_specs=P(("groups", "outer", "inner"), None),
        check_vma=False,
    )
```

time: 41.1 us -> 22.1 us (0.54)
  blocking collectives: 16.8 us -> 0 us
  local copies, waits for them, and re-layouts: 6.46 us -> 1.31 us
  Pallas kernels: 16.7 us -> 20.6 us
  other arithmetic: 0.68 us -> 0 us
    all_gather x1 -> x0, blocking collectives: 16.8 us -> none  [on_device(): lax.all_gather(jnp.stack([duty_codes, dwell_counts]), axes, axis=1, tiled...]
    broadcast_in_dim x7 -> x0, local copies, waits for them, and re-layouts: 5.1 us -> none  [the longest x1 0.79 us: on_device(): drive_on[:, None]]
    pallas_call x1, Pallas kernels: 16.7 us -> 20.6 us  [on_device(): pl.pallas_call(functools.partial(replay, axes, local), out_shape=jax.Shap...]
    unnamed x1 -> x0, other arithmetic: 0.68 us -> none
    unnamed x3 -> x1, local copies, waits for them, and re-layouts: 1.36 us -> 1.31 us
where the time goes in v2:
time: 22.1 us; the launch traced here: 21.9 us
  Pallas kernels  20.6 us (93%)
  local copies, waits for them, and re-layouts  1.31 us (6%)
    pallas_call x1, Pallas kernels, on_device(): pl.pallas_call(functools.partial(replay, axes, local), out_shape=jax.Shap...  20.6 us
    unnamed x1, local copies, waits for them, and re-layouts  1.31 us

profile of v2, /device:TPU:31, one launch (start us, length us, event | category | flops | bytes accessed | tf_op | source)
XLA Modules:
  0.0 21.9 jit_solution(956755285047353366)
XLA Ops:
  0.0 20.6 %shard_map.73 = f32[8,384]{1,0:T(8,128)} custom-call(s32[8]{0:T(128)} %duty.1, s32[8]{0:T(128)} %dwell.1, f32[384]{0:T(512)} %x0.1, f32[2,384,384]{2,1,0:T(8,128)} %coupling_hbm.1, f32[384]{0:T(512)} %decay.1, f32[384]{0:T(512)} %on.1, f32[384]{0:T(512)} %off.1), custom_call_target="tpu_custom_call" | custom-call | tf_op jit(solution)/shard_map/pallas_call | solution.py:170
  20.6 1.3 %copy.9 = f32[8,384]{1,0:T(8,128)} copy(f32[8,384]{1,0:T(8,128)} %shard_map.73) | data formatting | bytes 24576

commit v3 on v2

v3 whole, which is shorter than its diff:
```python
import functools
import jax
import jax.numpy as jnp
from jax import lax
from jax.experimental import pallas as pl
from jax.experimental.pallas import tpu as pltpu
from jax.sharding import PartitionSpec as P

DUTY_LEVELS = 16
DWELL_MAX = 8
LANES = 128
SUB = 8


def replay(axes, local, duty, dwell, x0, coupling_hbm, decay, on, off, out,
           drive_out, plus, turned, keep_col, keep_row, drive_row, mixed_on, mixed_off, coupling, packed, landed,
           codes, send_sem, recv_sem, coupling_sem, codes_sem):
    width = x0.shape[0]
    blocks = width // LANES
    inner = lax.axis_size(axes[1])
    count = lax.axis_size(axes[0]) * inner
    me = lax.axis_index(axes)

    def place_of(index):
        return {axes[0]: index // inner, axes[1]: index % inner}

    def push(target):
        return pltpu.make_async_remote_copy(
            src_ref=packed, dst_ref=landed.at[me], send_sem=send_sem.at[target], recv_sem=recv_sem.at[me],
            device_id=place_of(target), device_id_type=pl.DeviceIdType.MESH)

    barrier = pltpu.get_barrier_semaphore()

    def greet(source, unused):
        pl.semaphore_signal(barrier, inc=1, device_id=place_of(source), device_id_type=pl.DeviceIdType.MESH)
        return 0

    lax.fori_loop(0, me, greet, 0)
    load = pltpu.make_async_copy(coupling_hbm, coupling, coupling_sem)
    load.start()
    lane = lax.broadcasted_iota(jnp.int32, (1, LANES), 1)
    line = jnp.zeros((1, LANES), jnp.int32)
    for step in range(local):
        line = jnp.where(lane == step, duty[step], line)
        line = jnp.where(lane == local + step, dwell[step], line)
    packed[...] = line
    landed[me] = line

    @pl.when(me < count - 1)
    def to_later():
        pl.semaphore_wait(barrier, count - 1 - me)

        def send(target, unused):
            push(target).start()
            return 0

        lax.fori_loop(me + 1, count, send, 0)

    diag = (lax.broadcasted_iota(jnp.int32, (LANES, LANES), 0)
            == lax.broadcasted_iota(jnp.int32, (LANES, LANES), 1))
    per = LANES // SUB
    tiles = [slice(LANES * k, LANES * (k + 1)) for k in range(blocks)]
    groups = [slice(SUB * r, SUB * (r + 1)) for r in range(width // SUB)]

    def column(row, k):
        return jnp.sum(jnp.where(diag, row[:, tiles[k]], 0.0), axis=1, keepdims=True)

    decay_row, on_row, off_row = (ref[...].reshape(1, width) for ref in (decay, on, off))
    for level in range(DWELL_MAX + 1):
        keep_row[level] = jnp.broadcast_to(jnp.exp(-float(level) * decay_row), (SUB, width))
    for k in range(blocks):
        rates = column(decay_row, k)
        for level in range(DWELL_MAX + 1):
            keep_col[level, tiles[k]] = jnp.broadcast_to(jnp.exp(-float(level) * rates), (LANES, LANES))
    load.wait()

    totals = [[[None] * blocks for side in range(2)] for source in range(2)]
    for k in range(blocks):
        sources = (column(on_row, k), column(off_row, k))
        for side in range(2):
            for q in range(blocks):
                square = coupling[side, tiles[k], tiles[q]]
                for source in range(2):
                    folded = jnp.sum((square * sources[source]).reshape(per, SUB, LANES), axis=0)
                    old = totals[source][side][q]
                    totals[source][side][q] = folded if old is None else old + folded

    def through(source, side):
        return -jnp.concatenate([jnp.sum(t, axis=0, keepdims=True) for t in totals[source][side]], axis=1)

    through_on = [through(0, side) for side in range(2)]
    through_off = [through(1, side) for side in range(2)]

    def tabulate_duty(level, unused):
        frac = (level.astype(jnp.float32) + 0.5) / DUTY_LEVELS
        for k in range(blocks):
            for q in range(blocks):
                mixing = frac * coupling[0, tiles[k], tiles[q]] + (1.0 - frac) * coupling[1, tiles[k], tiles[q]]
                if k == q:
                    eye = jnp.where(diag, 1.0, 0.0)
                    plus[level, tiles[k], tiles[q]] = eye + mixing
                    turned[level, tiles[k]] = mixing - eye
                else:
                    plus[level, tiles[k], tiles[q]] = mixing
        drive_row[level] = jnp.broadcast_to(frac * on_row + (1.0 - frac) * off_row, (SUB, width))
        mixed_on[level] = jnp.broadcast_to(
            on_row + frac * through_on[0] + (1.0 - frac) * through_on[1], (SUB, width))
        mixed_off[level] = jnp.broadcast_to(
            off_row + frac * through_off[0] + (1.0 - frac) * through_off[1], (SUB, width))
        return 0

    lax.fori_loop(0, DUTY_LEVELS, tabulate_duty, 0)

    def unload(owner):
        return pltpu.make_async_copy(landed.at[owner], codes.at[owner], codes_sem.at[owner])

    def receive(source):
        @pl.when(source < me)
        def arrive():
            pltpu.make_async_remote_copy(
                src_ref=packed, dst_ref=landed.at[source], send_sem=send_sem.at[me], recv_sem=recv_sem.at[source],
                device_id=place_of(source), device_id_type=pl.DeviceIdType.MESH).wait_recv()

    def two_steps(owner, first, state, kept=None):
        duty_a, duty_b = codes[owner, 0, first], codes[owner, 0, first + 1]
        dwell_a, dwell_b = codes[owner, 0, local + first], codes[owner, 0, local + first + 1]
        frac_a = (duty_a.astype(jnp.float32) + 0.5) / DUTY_LEVELS
        scale_a = dwell_a.astype(jnp.float32) / DWELL_MAX
        scale_b = dwell_b.astype(jnp.float32) / DWELL_MAX
        sums = [[None, None] for k in range(blocks)]
        columns = []
        for r, rows in enumerate(groups):
            term = plus[duty_a, rows, tiles[0]] * state[:, tiles[0]]
            for k in range(1, blocks):
                term = term + plus[duty_a, rows, tiles[k]] * state[:, tiles[k]]
            middle = keep_col[dwell_a, rows] * jnp.sum(term, axis=1, keepdims=True)
            if kept is not None:
                columns.append(middle)
            for k in range(blocks):
                if k == r // per:
                    term = turned[duty_b, rows] * middle
                else:
                    term = plus[duty_b, rows, tiles[k]] * middle
                sums[k][r % 2] = term if sums[k][r % 2] is None else sums[k][r % 2] + term
        flat = jnp.concatenate([jnp.sum(s[0] + s[1], axis=0, keepdims=True) for s in sums], axis=1)
        driven = scale_a * (frac_a * mixed_on[duty_b] + (1.0 - frac_a) * mixed_off[duty_b])
        after = keep_row[dwell_b] * (driven - jnp.broadcast_to(flat, (SUB, width)))
        push_b = scale_b * drive_row[duty_b]
        if kept is None:
            return after + push_b
        row = lax.broadcasted_iota(jnp.int32, (local, width), 0)
        flat = jnp.concatenate([
            jnp.sum(jnp.where(diag, jnp.concatenate(columns[per * k:per * (k + 1)], axis=0), 0.0),
                    axis=0, keepdims=True) for k in range(blocks)], axis=1)
        states = jnp.where(row == first, flat, jnp.where(row == first + 1, after[0:1], kept[0]))
        drives = jnp.where(row == first, scale_a * drive_row[duty_a, 0:1],
                           jnp.where(row == first + 1, push_b[0:1], kept[1]))
        return after + push_b, (states, drives)

    half = local // 2
    state = jnp.broadcast_to(x0[...].reshape(1, width), (SUB, width))
    receive(0)
    unload(0).start()

    def block(owner, state):
        receive(owner + 1)
        unload(owner + 1).start()
        unload(owner).wait()
        return lax.fori_loop(0, half, lambda pair, state: two_steps(owner, 2 * pair, state), state)

    state = lax.fori_loop(0, me, block, state)
    unload(me).wait()
    blank = jnp.zeros((local, width), jnp.float32)
    state, kept = lax.fori_loop(
        0, half, lambda pair, carry: two_steps(me, 2 * pair, *carry), (state, (blank, blank)))
    out[...], drive_out[...] = kept

    def finish(target, unused):
        push(target).wait_send()
        return 0

    lax.fori_loop(me + 1, count, finish, 0)


def on_device(initial_state, duty_codes, dwell_counts, coupling, decay_rates, drive_on, drive_off):
    width, local = initial_state.shape[0], duty_codes.shape[0]
    axes = ("outer", "inner")
    count = lax.axis_size(axes[0]) * lax.axis_size(axes[1])
    scratch = [
        pltpu.VMEM((DUTY_LEVELS, width, width), jnp.float32),
        pltpu.VMEM((DUTY_LEVELS, width, LANES), jnp.float32),
        pltpu.VMEM((DWELL_MAX + 1, width, LANES), jnp.float32),
        pltpu.VMEM((DWELL_MAX + 1, SUB, width), jnp.float32),
        pltpu.VMEM((DUTY_LEVELS, SUB, width), jnp.float32),
        pltpu.VMEM((DUTY_LEVELS, SUB, width), jnp.float32),
        pltpu.VMEM((DUTY_LEVELS, SUB, width), jnp.float32),
        pltpu.VMEM(coupling.shape, jnp.float32),
        pltpu.VMEM((1, LANES), jnp.int32),
        pltpu.VMEM((count, 1, LANES), jnp.int32),
        pltpu.SMEM((count, 1, LANES), jnp.int32),
        pltpu.SemaphoreType.DMA((count,)),
        pltpu.SemaphoreType.DMA((count,)),
        pltpu.SemaphoreType.DMA,
        pltpu.SemaphoreType.DMA((count,)),
    ]
    smem, vmem = pl.BlockSpec(memory_space=pltpu.SMEM), pl.BlockSpec(memory_space=pltpu.VMEM)
    states, drives = pl.pallas_call(
        functools.partial(replay, axes, local),
        out_shape=[jax.ShapeDtypeStruct((local, width), jnp.float32)] * 2,
        in_specs=[smem, smem, vmem, pl.BlockSpec(memory_space=pl.ANY), vmem, vmem, vmem],
        out_specs=[vmem, vmem],
        scratch_shapes=scratch,
        compiler_params=pltpu.CompilerParams(
            vmem_limit_bytes=56 * 2**20, collective_id=0, has_side_effects=True),
    )(duty_codes, dwell_counts, initial_state, coupling, decay_rates, drive_on, drive_off)
    return states + drives


def solution(mesh):
    return jax.shard_map(
        on_device,
        mesh=mesh,
        in_specs=(
            P("groups"),
            P(("groups", "outer", "inner")),
            P(("groups", "outer", "inner")),
            P(),
            P(),
            P(),
            P(),
        ),
        out_specs=P(("groups", "outer", "inner"), None),
        check_vma=False,
    )
```

time: 22.1 us -> 19.8 us (0.90)
  Pallas kernels: 20.6 us -> 18.2 us
  other arithmetic: 0 us -> 1.33 us
  local copies, waits for them, and re-layouts: 1.31 us -> 0 us
    pallas_call x1, Pallas kernels: 20.6 us -> 18.2 us  [on_device(): pl.pallas_call(functools.partial(replay, axes, local), out_shape=[jax.Sha...]
    add x0 -> x1, other arithmetic: none -> 1.33 us  [on_device(): return states + drives]
    unnamed x1 -> x0, local copies, waits for them, and re-layouts: 1.31 us -> none
where the time goes in v3:
time: 19.8 us; the launch traced here: 19.5 us
  Pallas kernels  18.2 us (92%)
  other arithmetic  1.33 us (7%)
    pallas_call x1, Pallas kernels, on_device(): pl.pallas_call(functools.partial(replay, axes, local), out_shape=[jax.Sha...  18.2 us
    add x1, other arithmetic, on_device(): return states + drives  1.33 us

profile of v3, /device:TPU:31, one launch (start us, length us, event | category | flops | bytes accessed | tf_op | source)
XLA Modules:
  0.0 19.5 jit_solution(4022319131524027679)
XLA Ops:
  0.0 18.2 %shard_map.73 = (f32[8,384]{1,0:T(8,128)}, f32[8,384]{1,0:T(8,128)}) custom-call(s32[8]{0:T(128)} %duty.1, s32[8]{0:T(128)} %dwell.1, f32[384]{0:T(512)} %x0.1, f32[2,384,384]{2,1,0:T(8,128)} %coupling_hbm.1, f32[384]{0:T(512)} %decay.1, f32[384]{0:T(512)} %on.1, f32[384]{0:T(512)} %off.1), custom_call_target="tpu_custom_call" | custom-call | tf_op jit(solution)/shard_map/pallas_call | solution.py:207
  18.2 1.3 %add.3 = f32[8,384]{1,0:T(8,128)} add(f32[8,384]{1,0:T(8,128)} %get-tuple-element.7, f32[8,384]{1,0:T(8,128)} %get-tuple-element.8) | non-fusion elementwise | flops 3072 | bytes 36864 | tf_op jit(solution)/shard_map/add | solution.py:216

commit v4 on v3

--- a/solution.py
+++ b/solution.py
@@ -12,9 +12,9 @@
 SUB = 8
 
 
-def replay(axes, local, duty, dwell, x0, coupling_hbm, decay, on, off, out,
+def replay(axes, local, duty_hbm, dwell_hbm, x0_hbm, coupling_hbm, decay_hbm, on_hbm, off_hbm, out,
            drive_out, plus, turned, keep_col, keep_row, drive_row, mixed_on, mixed_off, coupling, packed, landed,
-           codes, send_sem, recv_sem, coupling_sem, codes_sem):
+           codes, send_sem, recv_sem, coupling_sem, codes_sem, duty, dwell, x0, decay, on, off, small_sem):
     width = x0.shape[0]
     blocks = width // LANES
     inner = lax.axis_size(axes[1])
@@ -37,7 +37,13 @@
 
     lax.fori_loop(0, me, greet, 0)
     load = pltpu.make_async_copy(coupling_hbm, coupling, coupling_sem)
+    pairs = ((duty_hbm, duty), (dwell_hbm, dwell), (decay_hbm, decay), (on_hbm, on), (off_hbm, off), (x0_hbm, x0))
+    loads = [pltpu.make_async_copy(a, b, small_sem.at[i]) for i, (a, b) in enumerate(pairs)]
+    for copy in loads:
+        copy.start()
     load.start()
+    for copy in loads[:2]:
+        copy.wait()
     lane = lax.broadcasted_iota(jnp.int32, (1, LANES), 1)
     line = jnp.zeros((1, LANES), jnp.int32)
     for step in range(local):
@@ -65,6 +71,8 @@
     def column(row, k):
         return jnp.sum(jnp.where(diag, row[:, tiles[k]], 0.0), axis=1, keepdims=True)
 
+    for copy in loads[2:]:
+        copy.wait()
     decay_row, on_row, off_row = (ref[...].reshape(1, width) for ref in (decay, on, off))
     for level in range(DWELL_MAX + 1):
         keep_row[level] = jnp.broadcast_to(jnp.exp(-float(level) * decay_row), (SUB, width))
@@ -202,12 +210,19 @@
         pltpu.SemaphoreType.DMA((count,)),
         pltpu.SemaphoreType.DMA,
         pltpu.SemaphoreType.DMA((count,)),
+        pltpu.SMEM((local,), jnp.int32),
+        pltpu.SMEM((local,), jnp.int32),
+        pltpu.VMEM((width,), jnp.float32),
+        pltpu.VMEM((width,), jnp.float32),
+        pltpu.VMEM((width,), jnp.float32),
+        pltpu.VMEM((width,), jnp.float32),
+        pltpu.SemaphoreType.DMA((6,)),
     ]
-    smem, vmem = pl.BlockSpec(memory_space=pltpu.SMEM), pl.BlockSpec(memory_space=pltpu.VMEM)
+    vmem = pl.BlockSpec(memory_space=pltpu.VMEM)
     states, drives = pl.pallas_call(
         functools.partial(replay, axes, local),
         out_shape=[jax.ShapeDtypeStruct((local, width), jnp.float32)] * 2,
-        in_specs=[smem, smem, vmem, pl.BlockSpec(memory_space=pl.ANY), vmem, vmem, vmem],
+        in_specs=[pl.BlockSpec(memory_space=pl.ANY)] * 7,
         out_specs=[vmem, vmem],
         scratch_shapes=scratch,
         compiler_params=pltpu.CompilerParams(

time: 19.8 us -> 19 us (0.960)
  Pallas kernels: 18.2 us -> 17.4 us
    pallas_call x1, Pallas kernels: 18.2 us -> 17.4 us  [on_device(): pl.pallas_call(functools.partial(replay, axes, local), out_shape=[jax.Sha...]
where the time goes in v4:
time: 19 us; the launch traced here: 18.8 us
  Pallas kernels  17.4 us (92%)
  other arithmetic  1.33 us (7%)
    pallas_call x1, Pallas kernels, on_device(): pl.pallas_call(functools.partial(replay, axes, local), out_shape=[jax.Sha...  17.4 us
    add x1, other arithmetic, on_device(): return states + drives  1.33 us

profile of v4, /device:TPU:31, one launch (start us, length us, event | category | flops | bytes accessed | tf_op | source)
XLA Modules:
  0.0 18.8 jit_solution(1711117898277164170)
XLA Ops:
  0.0 17.4 %shard_map.73 = (f32[8,384]{1,0:T(8,128)}, f32[8,384]{1,0:T(8,128)}) custom-call(s32[8]{0:T(128)} %duty_hbm.1, s32[8]{0:T(128)} %dwell_hbm.1, f32[384]{0:T(512)} %x0_hbm.1, f32[2,384,384]{2,1,0:T(8,128)} %coupling_hbm.1, f32[384]{0:T(512)} %decay_hbm.1, f32[384]{0:T(512)} %on_hbm.1, f32[384]{0:T(512)} %off_hbm.1), custom_call_target="tpu_custom_call" | custom-call | tf_op jit(solution)/shard_map/pallas_call | solution.py:222
  17.4 1.3 %add.3 = f32[8,384]{1,0:T(8,128)} add(f32[8,384]{1,0:T(8,128)} %get-tuple-element.7, f32[8,384]{1,0:T(8,128)} %get-tuple-element.8) | non-fusion elementwise | flops 3072 | bytes 36864 | tf_op jit(solution)/shard_map/add | solution.py:231

commit v5 on v4

--- a/solution.py
+++ b/solution.py
@@ -13,7 +13,7 @@
 
 
 def replay(axes, local, duty_hbm, dwell_hbm, x0_hbm, coupling_hbm, decay_hbm, on_hbm, off_hbm, out,
-           drive_out, plus, turned, keep_col, keep_row, drive_row, mixed_on, mixed_off, coupling, packed, landed,
+           plus, turned, keep_col, keep_row, drive_row, mixed_on, mixed_off, coupling, packed, landed,
            codes, send_sem, recv_sem, coupling_sem, codes_sem, duty, dwell, x0, decay, on, off, small_sem):
     width = x0.shape[0]
     blocks = width // LANES
@@ -160,10 +160,9 @@
         flat = jnp.concatenate([
             jnp.sum(jnp.where(diag, jnp.concatenate(columns[per * k:per * (k + 1)], axis=0), 0.0),
                     axis=0, keepdims=True) for k in range(blocks)], axis=1)
-        states = jnp.where(row == first, flat, jnp.where(row == first + 1, after[0:1], kept[0]))
-        drives = jnp.where(row == first, scale_a * drive_row[duty_a, 0:1],
-                           jnp.where(row == first + 1, push_b[0:1], kept[1]))
-        return after + push_b, (states, drives)
+        after = after + push_b
+        flat = flat + scale_a * drive_row[duty_a, 0:1]
+        return after, jnp.where(row == first, flat, jnp.where(row == first + 1, after[0:1], kept))
 
     half = local // 2
     state = jnp.broadcast_to(x0[...].reshape(1, width), (SUB, width))
@@ -180,8 +179,8 @@
     unload(me).wait()
     blank = jnp.zeros((local, width), jnp.float32)
     state, kept = lax.fori_loop(
-        0, half, lambda pair, carry: two_steps(me, 2 * pair, *carry), (state, (blank, blank)))
-    out[...], drive_out[...] = kept
+        0, half, lambda pair, carry: two_steps(me, 2 * pair, *carry), (state, blank))
+    out[...] = kept
 
     def finish(target, unused):
         push(target).wait_send()
@@ -219,16 +218,15 @@
         pltpu.SemaphoreType.DMA((6,)),
     ]
     vmem = pl.BlockSpec(memory_space=pltpu.VMEM)
-    states, drives = pl.pallas_call(
+    return pl.pallas_call(
         functools.partial(replay, axes, local),
-        out_shape=[jax.ShapeDtypeStruct((local, width), jnp.float32)] * 2,
+        out_shape=jax.ShapeDtypeStruct((local, width), jnp.float32),
         in_specs=[pl.BlockSpec(memory_space=pl.ANY)] * 7,
-        out_specs=[vmem, vmem],
+        out_specs=vmem,
         scratch_shapes=scratch,
         compiler_params=pltpu.CompilerParams(
             vmem_limit_bytes=56 * 2**20, collective_id=0, has_side_effects=True),
     )(duty_codes, dwell_counts, initial_state, coupling, decay_rates, drive_on, drive_off)
-    return states + drives
 
 
 def solution(mesh):

time: 19 us -> 19 us (level)
  other arithmetic: 1.33 us -> 0 us
  local copies, waits for them, and re-layouts: 0 us -> 1.31 us
    add x1 -> x0, other arithmetic: 1.33 us -> none  [on_device(): return states + drives]
    unnamed x0 -> x1, local copies, waits for them, and re-layouts: none -> 1.31 us
where the time goes in v5:
time: 19 us; the launch traced here: 18.7 us
  Pallas kernels  17.4 us (92%)
  local copies, waits for them, and re-layouts  1.31 us (7%)
    pallas_call x1, Pallas kernels, on_device(): pl.pallas_call(functools.partial(replay, axes, local), out_shape=jax.Shap...  17.4 us
    unnamed x1, local copies, waits for them, and re-layouts  1.31 us

profile of v5, /device:TPU:31, one launch (start us, length us, event | category | flops | bytes accessed | tf_op | source)
XLA Modules:
  0.0 18.7 jit_solution(14098822793304965011)
XLA Ops:
  0.0 17.4 %shard_map.73 = f32[8,384]{1,0:T(8,128)} custom-call(s32[8]{0:T(128)} %duty_hbm.1, s32[8]{0:T(128)} %dwell_hbm.1, f32[384]{0:T(512)} %x0_hbm.1, f32[2,384,384]{2,1,0:T(8,128)} %coupling_hbm.1, f32[384]{0:T(512)} %decay_hbm.1, f32[384]{0:T(512)} %on_hbm.1, f32[384]{0:T(512)} %off_hbm.1), custom_call_target="tpu_custom_call" | custom-call | tf_op jit(solution)/shard_map/pallas_call | solution.py:221
  17.4 1.3 %copy.9 = f32[8,384]{1,0:T(8,128)} copy(f32[8,384]{1,0:T(8,128)} %shard_map.73) | data formatting | bytes 24576
